TPU v7x, 32 devices: a whole 2x2x4 slice. The times are simulated.
32 devices in a mesh: parts: 2 (over y), tp: 4 (over z), section: 4 (over x, core).
Axes of the slice: x: 2, y: 2, z: 4, core: 2. Of those that a mesh axis runs over, the one named last changes fastest.
Arguments:
- memory: bfloat16 [8, 1024, 8192], P('parts', 'tp'), parts along dimension 0, may hold values from -6 to 6
- mem_lengths: int32 [8], P('parts'), parts along dimension 0, may hold values from 128 to 1024, as said below
- decode_group: int32 [8], P('parts'), parts along dimension 0, may hold values from 0 to 3, as said below
- row_counts: int32 [8], P('parts'), parts along dimension 0, may hold values from 1 to 32, as said below
- hidden: bfloat16 [16, 32, 8192], P(('parts', 'section')), parts along dimension 0, may hold values from -6 to 6
- norm_gain: bfloat16 [8192], replicated, may hold values from 0.5 to 1.5
- q_weight: bfloat16 [8192, 8192], P('section', 'tp'), may hold values from -0.0625 to 0.0625
- k_weight: bfloat16 [8192, 1024], P('tp', 'section'), may hold values from -0.0625 to 0.0625
- v_weight: bfloat16 [8192, 1024], P('tp', 'section'), may hold values from -0.0625 to 0.0625
- q_gain: float32 [128], replicated, may hold values from 0.5 to 1.5
- k_gain: float32 [128], replicated, may hold values from 0.5 to 1.5
- o_weight: bfloat16 [8192, 8192], P('tp', 'section'), may hold values from -0.25 to 0.25
Outputs:
- updated: bfloat16 [16, 32, 8192], P(('parts', 'section')), parts along dimension 0
There are 2 independent parts, one for each index of `parts`. A program takes and returns all parts, laid end to end along the dimension named above; an argument that names none is the same for every part. Nothing has to cross between parts.
Inputs may be any that keep to these rules, and one draw needn't show every extreme that they name: `decode_group`: each group is named by at most 2 requests, and some group by exactly 2. `mem_lengths`: multiples of 128; some request has exactly 128 and another exactly 1024. `row_counts`: some request has exactly 32.
All inputs are finite; a program needn't handle non-finite values.
Results may differ from a plain program's by a relative error of at most 0.005.
Values may be sent and summed in bfloat16 or wider, within the bound.
A program may use at most 320 MiB of HBM per device.

v0:
```python
import jax
import jax.numpy as jnp
from jax import lax
from jax.sharding import PartitionSpec as P

KVH = 8
HD = 128
STEPS = 2
GROUP = 8


EPSILON = 1e-06


def head_norm(values_in, gain_vector):
    return (
        values_in
        * lax.rsqrt(jnp.mean(values_in * values_in, axis=-1, keepdims=True) + EPSILON)
        * gain_vector
    )


def slot_onehot(decode_group, groups, capacity):
    total = decode_group.shape[0]
    ordinal = jnp.arange(total, dtype=jnp.int32)
    matches = decode_group[None, :] == decode_group[:, None]
    slot_rank = jnp.sum((matches & (ordinal[None, :] < ordinal[:, None])).astype(jnp.int32), axis=1)
    group_ids = jnp.arange(groups, dtype=jnp.int32)
    slot_ids = jnp.arange(capacity, dtype=jnp.int32)
    chosen = (decode_group[None, None, :] == group_ids[:, None, None]) & (
        slot_rank[None, None, :] == slot_ids[None, :, None]
    )
    return chosen.astype(jnp.float32)


def body(
    memory,
    mem_lengths,
    decode_group,
    row_counts,
    hidden,
    norm_gain,
    q_weight,
    k_weight,
    v_weight,
    q_gain,
    k_gain,
    o_weight,
):
    tp_count = lax.axis_size("tp")
    section_count = lax.axis_size("section")
    req_count, tok_local, model_width = memory.shape
    capacity, row_count = (hidden.shape[0], hidden.shape[1])
    heads_local = q_weight.shape[1] // HD
    section_heads = k_weight.shape[1] // HD
    kv_local = max(1, heads_local // GROUP)
    per_kv = heads_local // kv_local
    mem_len = tok_local * tp_count
    mem_rows = memory.reshape(req_count * tok_local, model_width)
    key_acc = jnp.dot(
        mem_rows,
        lax.all_gather(k_weight, "tp", axis=0, tiled=True),
        preferred_element_type=jnp.float32,
    )
    value_acc = jnp.dot(
        mem_rows,
        lax.all_gather(v_weight, "tp", axis=0, tiled=True),
        preferred_element_type=jnp.float32,
    )
    key_heads = head_norm(key_acc.reshape(req_count, tok_local, section_heads, HD), k_gain).astype(
        jnp.bfloat16
    )
    value_heads = value_acc.reshape(req_count, tok_local, section_heads, HD).astype(jnp.bfloat16)
    packed = jnp.stack([key_heads, value_heads], axis=2)
    slot_map = slot_onehot(decode_group, section_count, capacity)
    outgoing = jnp.einsum(
        "gcr,rtvjd->gjctvd",
        slot_map.astype(jnp.bfloat16),
        packed,
        preferred_element_type=jnp.float32,
    ).astype(jnp.bfloat16)
    by_head = lax.all_to_all(outgoing, "section", split_axis=0, concat_axis=1, tiled=True)[0]
    repeat_count = tp_count * kv_local // KVH
    grouped = by_head.reshape(KVH // kv_local, kv_local, capacity, tok_local, 2, HD)
    spread = jnp.repeat(grouped, repeat_count, axis=0)
    mine = lax.all_to_all(spread, "tp", split_axis=0, concat_axis=3, tiled=True)[0]
    keys_mine = mine[:, :, :, 0, :]
    values_mine = mine[:, :, :, 1, :]
    q_full, o_full = (
        lax.all_gather(q_weight, "section", axis=0, tiled=True),
        lax.all_gather(o_weight, "section", axis=1, tiled=True),
    )
    group_index = lax.axis_index("section")
    my_slots = lax.dynamic_index_in_dim(slot_map, group_index, 0, keepdims=False)
    occupied = jnp.sum(my_slots, axis=1)
    key_len = (
        jnp.sum(my_slots * mem_lengths.astype(jnp.float32)[None, :], axis=1)
        + (1.0 - occupied) * mem_len
    )
    live_count = jnp.sum(my_slots * row_counts.astype(jnp.float32)[None, :], axis=1)
    key_mask = (jnp.arange(mem_len, dtype=jnp.float32)[None, :] < key_len[:, None]).astype(
        jnp.float32
    )
    row_live = (jnp.arange(row_count, dtype=jnp.float32)[None, :] < live_count[:, None]).astype(
        jnp.float32
    )
    state = hidden
    for step_index in range(STEPS):
        state_f32 = state.astype(jnp.float32)
        normed = (
            state_f32
            * lax.rsqrt(jnp.mean(state_f32 * state_f32, axis=-1, keepdims=True) + EPSILON)
            * norm_gain.astype(jnp.float32)
        ).astype(jnp.bfloat16)
        queries = jnp.dot(
            normed.reshape(capacity * row_count, model_width),
            q_full,
            preferred_element_type=jnp.float32,
        )
        queries = queries.reshape(capacity, row_count, kv_local, per_kv, HD)
        queries = (head_norm(queries, q_gain) * HD ** (-0.5)).astype(jnp.bfloat16)
        scores = jnp.einsum(
            "crkgd,kcld->crkgl", queries, keys_mine, preferred_element_type=jnp.float32
        )
        raw = jnp.exp(scores) * key_mask[:, None, None, None, :]
        softmax = (raw / jnp.sum(raw, axis=-1, keepdims=True)).astype(jnp.bfloat16)
        attended = jnp.einsum(
            "crkgl,kcld->crkgd", softmax, values_mine, preferred_element_type=jnp.float32
        )
        attended = attended.astype(jnp.bfloat16).reshape(capacity * row_count, heads_local * HD)
        branch = lax.psum(jnp.dot(attended, o_full, preferred_element_type=jnp.float32), "tp")
        state = (
            state_f32 + row_live[:, :, None] * branch.reshape(capacity, row_count, model_width)
        ).astype(jnp.bfloat16)
    return state


def solution(mesh):
    in_specs = (
        P("parts", "tp", None),
        P("parts"),
        P("parts"),
        P("parts"),
        P(("parts", "section"), None, None),
        P(),
        P("section", "tp"),
        P("tp", "section"),
        P("tp", "section"),
        P(),
        P(),
        P("tp", "section"),
    )
    out_specs = P(("parts", "section"), None, None)
    return jax.shard_map(body, mesh=mesh, in_specs=in_specs, out_specs=out_specs, check_vma=False)
```

profile of v0, /device:TPU:0, one launch (start us, length us, event | category | flops | bytes accessed | tf_op | source)
XLA Modules:
  0.0 832.3 jit_solution(17360762830353144371)
XLA Ops:
  6.5 0.7 all-gather.5.cloned.1.call-update
  7.3 0.7 all-gather.7.cloned.1.call-update
  8.1 0.7 all-gather.9.cloned.1.call-update
  8.8 0.5 all-gather.11.cloned.1.call-update
  9.6 82.8 %all-gather.5.cloned.1.call-done = bf16[8192,256]{1,0:T(8,128)(2,1)} async-done(((bf16[2048,256]{1,0:T(8,128)(2,1)}), bf16[8192,256]{1,0:T(8,128)(2,1)}) %all-gather.5.cloned.1.call-update) | async-done | bytes 4194320 | tf_op jit(solution)/shard_map/all_gather | solution.py:62
  92.4 6.4 copy.30
  98.8 74.5 %all-gather.7.cloned.1.call-done = bf16[8192,256]{1,0:T(8,128)(2,1)} async-done(((bf16[2048,256]{1,0:T(8,128)(2,1)}), bf16[8192,256]{1,0:T(8,128)(2,1)}) %all-gather.7.cloned.1.call-update) | async-done | bytes 4194320 | tf_op jit(solution)/shard_map/all_gather | solution.py:67
  173.3 6.4 copy.31
  179.7 14.6 %multiply_reduce_fusion = (f32[4,256,2]{1,2,0:T(2,128)S(1)}, f32[4,256,2,128]{1,3,2,0:T(8,128)S(1)}) fusion(bf16[2,128,8192,1]{2,1,0,3:T(8,128)(2,1)} %bitcast.132, bf16[4,256,8192]{2,1,0:T(8,128)(2,1)} %param.12), kind=kOutput, calls=%fused_computation.47 | convolution fusion | flops 4295489536 | bytes 22028288 | tf_op jit(solution)/shard_map/dot_general | solution.py:60
  194.5 10.9 %fusion.21 = bf16[4,256,1,2,128]{1,4,3,0,2:T(8,128)(2,1)S(1)} fusion(bf16[2,128,8192,1]{2,1,0,3:T(8,128)(2,1)S(1)} %bitcast.131, bf16[4,256,8192]{2,1,0:T(8,128)(2,1)} %param.12), kind=kOutput, calls=%fused_computation.30 | convolution fusion | flops 4295229440 | bytes 21495808 | tf_op jit(solution)/shard_map/dot_general | solution.py:65
  205.5 1.1 copy.44
  206.6 1.2 convert_bitcast_fusion
  207.9 1.6 copy.35
  209.5 51.9 %all_to_all.24 = bf16[4,2,2,256,2,128]{5,2,1,4,3,0:T(2,128)(2,1)} all-to-all(bf16[4,2,2,256,2,128]{5,2,1,4,3,0:T(2,128)(2,1)S(1)} %copy.35), channel_id=1, replica_groups=mesh['parts'=2,'tp'=4,'section'=4] {'section'}, dimensions={0} | all-to-all | bytes 4194304 | tf_op jit(solution)/shard_map/all_to_all | solution.py:82
  261.4 4.4 all-to-all-start.1
  266.8 47.3 %all-to-all-done.1 = bf16[4,2,2,256,2,128]{5,2,1,4,3,0:T(2,128)(2,1)} async-done(((bf16[4,2,2,256,2,128]{5,2,1,4,3,0:T(2,128)(2,1)}), bf16[4,2,2,256,2,128]{5,2,1,4,3,0:T(2,128)(2,1)}, u32[]{:S(2)}, u32[]{:S(2)}) %all-to-all-start.1) | async-done | bytes 2097184 | tf_op jit(solution)/shard_map/all_to_all | solution.py:86
  314.1 3.4 copy.54
  317.5 80.0 %all-gather.9.cloned.1.call-done = bf16[8192,2048]{1,0:T(8,128)(2,1)} async-done(((bf16[2048,2048]{1,0:T(8,128)(2,1)}), bf16[8192,2048]{1,0:T(8,128)(2,1)}) %all-gather.9.cloned.1.call-update) | async-done | bytes 33554448 | tf_op jit(solution)/shard_map/all_gather | solution.py:90
  397.5 42.2 %copy.39 = bf16[2048,8192]{1,0:T(8,128)(2,1)} copy(bf16[2048,8192]{0,1:T(8,128)(2,1)} %bitcast.122) | data formatting | bytes 67108864 | tf_op jit(solution)/shard_map/dot_general | solution.py:115
  439.7 15.8 %multiply_reduce_fusion.2 = (f32[2,32,2,8]{1,3,2,0:T(8,128)S(1)}, f32[2,32,2,8,128]{4,1,3,2,0:T(8,128)S(1)}) fusion(bf16[2,8,128,8192,1]{3,2,1,0,4:T(8,128)(2,1)} %bitcast.120, bf16[2,32,8192]{2,1,0:T(8,128)(2,1)S(1)} %copy-done, f32[8192]{0:T(1024)S(1)} %convert_element_type.97, f32[2,32]{1,0:T(2,128)S(1)} %add_rsqrt_fusion.4), kind=kOutput, calls=%fused_computation.54 | convolution fusion | flops 2149841920 | bytes 35164416 | tf_op jit(solution)/shard_map/dot_general | solution.py:115
  455.6 1.2 bitcast_reduce_fusion.1
  456.7 0.9 fusion.30
  457.9 142.5 %all-gather.11.cloned.1.call-done = bf16[2048,8192]{1,0:T(8,128)(2,1)} async-done(((bf16[2048,2048]{1,0:T(8,128)(2,1)}), bf16[2048,8192]{1,0:T(8,128)(2,1)}) %all-gather.11.cloned.1.call-update) | async-done | bytes 33554448 | tf_op jit(solution)/shard_map/all_gather | solution.py:91
  600.4 14.9 %fusion.63 = f32[64,8192]{1,0:T(8,128)} fusion(bf16[64,2048]{1,0:T(8,128)(2,1)S(1)} %reshape.178, bf16[2048,8192]{1,0:T(8,128)(2,1)} %all-gather.11.cloned.1.call-done), kind=kOutput, calls=%fused_computation.85 | convolution fusion | flops 2147483648 | bytes 35913728 | tf_op jit(solution)/shard_map/dot_general | solution.py:131
  615.7 86.3 %all-reduce.3.cloned.1.call-done = f32[2,32,8192]{2,1,0:T(8,128)} async-done(((f32[2,32,8192]{2,1,0:T(8,128)}), f32[2,32,8192]{2,1,0:T(8,128)}) %all-reduce.3.cloned.1.call-update) | async-done | bytes 2097168 | tf_op jit(solution)/shard_map/psum | solution.py:131
  702.1 2.1 fusion.10
  704.2 15.5 %multiply_reduce_fusion.1 = (f32[2,32,2,8]{1,3,2,0:T(8,128)S(1)}, f32[2,32,2,8,128]{4,1,3,2,0:T(8,128)S(1)}) fusion(bf16[2,8,128,8192,1]{3,2,1,0,4:T(8,128)(2,1)} %bitcast.121, bf16[2,32,8192]{2,1,0:T(8,128)(2,1)S(1)} %get-tuple-element.8, f32[2,32]{1,0:T(2,128)S(1)} %add_rsqrt_fusion.3, f32[8192]{0:T(1024)S(1)} %convert_element_type.97), kind=kOutput, calls=%fused_computation.52 | convolution fusion | flops 2149841920 | bytes 35164416 | tf_op jit(solution)/shard_map/dot_general | solution.py:115
  719.7 1.2 bitcast_reduce_fusion
  720.9 0.9 fusion.33
  722.0 14.9 %fusion.64 = f32[64,8192]{1,0:T(8,128)} fusion(bf16[64,2048]{1,0:T(8,128)(2,1)S(1)} %reshape.180, bf16[2048,8192]{1,0:T(8,128)(2,1)} %all-gather.11.cloned.1.call-done), kind=kOutput, calls=%fused_computation.86 | convolution fusion | flops 2147483648 | bytes 35913728 | tf_op jit(solution)/shard_map/dot_general | solution.py:131
  737.0 85.6 %all-reduce.5.cloned.1.call-done = f32[2,32,8192]{2,1,0:T(8,128)} async-done(((f32[2,32,8192]{2,1,0:T(8,128)}), f32[2,32,8192]{2,1,0:T(8,128)}) %all-reduce.5.cloned.1.call-update) | async-done | bytes 2097168 | tf_op jit(solution)/shard_map/psum | solution.py:131
  822.6 2.9 fusion.13
  (52 shorter events, 2.4 us)
Async XLA Ops:
  6.5 85.9 %all-gather.5.cloned.1.call-start = ((), (), s32[]{:S(2)}) async-start(), calls=%async_computation.2 | async-start | bytes 5242880 | tf_op jit(solution)/shard_map/all_gather | solution.py:62
  7.3 166.1 %all-gather.7.cloned.1.call-start = ((), (), s32[]{:S(2)}) async-start(), calls=%async_computation.3 | async-start | bytes 5242880 | tf_op jit(solution)/shard_map/all_gather | solution.py:67
  8.0 389.5 %all-gather.9.cloned.1.call-start = ((), (), s32[]{:S(2)}) async-start(), calls=%async_computation.4 | async-start | bytes 41943040 | tf_op jit(solution)/shard_map/all_gather | solution.py:90
  8.7 0.7 copy-start.7
  8.8 591.7 %all-gather.11.cloned.1.call-start = ((), (), s32[]{:S(2)}) async-start(), calls=%async_computation.5 | async-start | bytes 41943040 | tf_op jit(solution)/shard_map/all_gather | solution.py:91
  179.7 14.7 %copy-start.6 = (f32[128]{0:T(128)S(1)}, f32[128]{0:T(128)}, u32[]{:S(2)}) copy-start(f32[128]{0:T(128)} %param.22) | copy-start | bytes 1540
  179.7 14.8 %copy-start.3 = (bf16[256,8192]{1,0:T(8,128)(2,1)S(1)}, bf16[256,8192]{1,0:T(8,128)(2,1)}, u32[]{:S(2)}) copy-start(bf16[256,8192]{1,0:T(8,128)(2,1)} %copy.31) | copy-start | bytes 12582916
  209.5 56.6 %copy-start.8 = (s32[4]{0:T(128)S(1)}, s32[4]{0:T(128)}, u32[]{:S(2)}) copy-start(s32[4]{0:T(128)} %param.13) | copy-start | bytes 52
  209.5 56.6 %copy-start.9 = (s32[4]{0:T(128)S(1)}, s32[4]{0:T(128)}, u32[]{:S(2)}) copy-start(s32[4]{0:T(128)} %param.15) | copy-start | bytes 52
  209.5 56.6 %copy-start.4 = (bf16[8192]{0:T(1024)(128)(2,1)S(1)}, bf16[8192]{0:T(1024)(128)(2,1)}, u32[]{:S(2)}) copy-start(bf16[8192]{0:T(1024)(128)(2,1)} %param.17) | copy-start | bytes 49156
  209.5 56.9 %copy-start = (bf16[2,32,8192]{2,1,0:T(8,128)(2,1)S(1)}, bf16[2,32,8192]{2,1,0:T(8,128)(2,1)}, u32[]{:S(2)}) copy-start(bf16[2,32,8192]{2,1,0:T(8,128)(2,1)} %param.16) | copy-start | bytes 3145732
  261.4 52.7 %all-to-all-start.1 = ((bf16[4,2,2,256,2,128]{5,2,1,4,3,0:T(2,128)(2,1)}), bf16[4,2,2,256,2,128]{5,2,1,4,3,0:T(2,128)(2,1)}, u32[]{:S(2)}, u32[]{:S(2)}) async-start(bf16[4,2,2,256,2,128]{5,2,1,4,3,0:T(2,128)(2,1)} %all_to_all.24), calls=%async_computation.1 | async-start | bytes 4194304 | tf_op jit(solution)/shard_map/all_to_all | solution.py:86
  265.8 436.2 %all-reduce.3.cloned.1.call-start = ((), (), s32[]{:S(2)}) async-start(), calls=%async_computation.6 | async-start | bytes 4194304 | tf_op jit(solution)/shard_map/psum | solution.py:131
  439.7 15.8 %copy-start.1 = (bf16[4,2,2,256,2,128]{5,3,0,1,2,4:T(8,128)(2,1)S(1)}, bf16[4,2,2,256,2,128]{5,3,0,1,2,4:T(8,128)(2,1)}, u32[]{:S(2)}) copy-start(bf16[4,2,2,256,2,128]{5,3,0,1,2,4:T(8,128)(2,1)} %copy.54) | copy-start | bytes 6291460
  439.7 15.8 %copy-start.5 = (f32[128]{0:T(128)S(1)}, f32[128]{0:T(128)}, u32[]{:S(2)}) copy-start(f32[128]{0:T(128)} %param.21) | copy-start | bytes 1540
  615.4 207.2 %all-reduce.5.cloned.1.call-start = ((), (), s32[]{:S(2)}) async-start(), calls=%async_computation.7 | async-start | bytes 4194304 | tf_op jit(solution)/shard_map/psum | solution.py:131
  704.2 15.5 %copy-start.2 = (bf16[4,2,2,256,2,128]{5,3,0,1,2,4:T(8,128)(2,1)S(1)}, bf16[4,2,2,256,2,128]{5,3,0,1,2,4:T(8,128)(2,1)}, u32[]{:S(2)}) copy-start(bf16[4,2,2,256,2,128]{5,3,0,1,2,4:T(8,128)(2,1)} %copy.54) | copy-start | bytes 6291460
Sparse Core Ops, SparseCore 0:
  8.9 83.4 all-gather.4
  94.0 79.2 all-gather.6
  174.9 222.5 all-gather.8
  398.9 201.4 all-gather.10
  615.5 86.5 all-reduce.2
  737.1 85.4 all-reduce.4
where the time goes:
time: 834 us; the launch traced here: 832 us
  waiting for transfers between devices  602 us (72%)
  matrix products  92 us (11%)
  local copies, waits for them, and re-layouts  61.6 us (7%)
  blocking collectives  51.9 us (6%)
  between operations  13.8 us (2%)
    psum x2, waiting for transfers between devices, body(): lax.psum(jnp.dot(attended, o_full, preferred_element_type=jnp.float32), '...  172 us
    all_gather x1, waiting for transfers between devices, body(): lax.all_gather(o_weight, 'section', axis=1, tiled=True)  143 us
    all_gather x1, waiting for transfers between devices, body(): lax.all_gather(k_weight, 'tp', axis=0, tiled=True)  82.8 us
    all_gather x1, waiting for transfers between devices, body(): lax.all_gather(q_weight, 'section', axis=0, tiled=True)  80 us
    all_gather x1, waiting for transfers between devices, body(): lax.all_gather(v_weight, 'tp', axis=0, tiled=True)  74.5 us
    all_to_all x1, blocking collectives, body(): lax.all_to_all(outgoing, 'section', split_axis=0, concat_axis=1, tiled=True)  51.9 us
    all_to_all x1, waiting for transfers between devices, body(): lax.all_to_all(spread, 'tp', split_axis=0, concat_axis=3, tiled=True)[0]  47.3 us
    dot_general x1, local copies, waits for them, and re-layouts, body(): jnp.dot(normed.reshape(capacity * row_count, model_width), q_full, prefer...  42.2 us
  transfers between devices with their start and end apart: 7, of which 7 were waited for; matrix products, arithmetic and copies ran while one was open for 13% of the time, Pallas kernels for 0%

commit v1 on v0

--- a/solution.py
+++ b/solution.py
@@ -1,6 +1,10 @@
+import functools
+
 import jax
 import jax.numpy as jnp
 from jax import lax
+from jax.experimental import pallas as pl
+from jax.experimental.pallas import tpu as pltpu
 from jax.sharding import PartitionSpec as P
 
 KVH = 8
@@ -10,6 +14,9 @@
 
 
 EPSILON = 1e-06
+MESH = pl.DeviceIdType.MESH
+TILE = 512
+VMEM_LIMIT = 58 * 1024 * 1024
 
 
 def head_norm(values_in, gain_vector):
@@ -31,6 +38,389 @@
         slot_rank[None, None, :] == slot_ids[None, :, None]
     )
     return chosen.astype(jnp.float32)
+
+
+def decode_kernel(
+    n,
+    lens_ref,
+    rows_ref,
+    map_ref,
+    hidden_ref,
+    gain_ref,
+    qgain_ref,
+    keys_ref,
+    values_ref,
+    qw_hbm,
+    ow_hbm,
+    out_ref,
+    qw,
+    ow,
+    xs,
+    hb,
+    st,
+    sq,
+    rq,
+    sn,
+    rn,
+    qn,
+    aq,
+    so,
+    ro,
+    sl,
+    rl,
+    at,
+    aa,
+    sb,
+    rb,
+    ob,
+    rob,
+    wsem,
+    hsem,
+    qsem,
+    nsem,
+    asem,
+    osem,
+    lsem,
+    gsem,
+    bsem,
+    ssem,
+    fsem,
+):
+    part = lax.axis_index("parts")
+    t = lax.axis_index("tp")
+    s = lax.axis_index("section")
+    cap, rows, width = hidden_ref.shape
+    block = width // n
+    toks = keys_ref.shape[1]
+    kv = keys_ref.shape[2] // HD
+    diag = s == t
+    sends = []
+
+    def remote(src, dst, sems, i_send, i_recv, tp, section):
+        return pltpu.make_async_remote_copy(
+            src_ref=src,
+            dst_ref=dst,
+            send_sem=sems.at[0].at[i_send],
+            recv_sem=sems.at[1].at[i_recv],
+            device_id=(part, tp, section),
+            device_id_type=MESH,
+        )
+
+    def send(*args):
+        copy = remote(*args)
+        copy.start()
+        sends.append((copy, None))
+
+    def send_or_keep(src, dst, *args):
+        copy = remote(src, dst, *args)
+
+        @pl.when(diag)
+        def _():
+            dst[...] = src[...]
+
+        @pl.when(jnp.logical_not(diag))
+        def _():
+            copy.start()
+
+        sends.append((copy, jnp.logical_not(diag)))
+
+    def receive(dst, sems, i):
+        remote(dst, dst, sems, i, i, t, s).wait_recv()
+
+    def receive_or_kept(dst, sems, i):
+        @pl.when(jnp.logical_not(diag))
+        def _():
+            receive(dst, sems, i)
+
+    def ring(me, d):
+        return lax.rem(me + d, n)
+
+    qcopy = pltpu.make_async_copy(qw_hbm, qw, wsem.at[0])
+    qcopy.start()
+    ocopy = pltpu.make_async_copy(ow_hbm, ow, wsem.at[1])
+    ocopy.start()
+
+    barrier = pltpu.get_barrier_semaphore()
+    for dt in range(n):
+        for ds in range(n):
+            if dt or ds:
+                pl.semaphore_signal(
+                    barrier, inc=1, device_id=(part, ring(t, dt), ring(s, ds)), device_id_type=MESH
+                )
+    pl.semaphore_wait(barrier, n * n - 1)
+
+    def columns(i):
+        return pl.ds(pl.multiple_of(i * block, block), block)
+
+    for d in range(1, n):
+        g = ring(s, d)
+        send(hidden_ref.at[:, :, columns(g)], hb.at[s], hsem, g, s, t, g)
+    hb[s] = hidden_ref[:, :, columns(s)]
+    for d in range(1, n):
+        g = ring(s, d)
+        receive(hb.at[g], hsem, g)
+    for r in range(n):
+        held = jnp.zeros((rows, block), jnp.float32)
+        for g in range(n):
+            for c in range(cap):
+                chosen = map_ref[g, c * n + r] > 0
+                held = jnp.where(chosen, hb[g, c].astype(jnp.float32), held)
+        st[0, r] = held.astype(jnp.bfloat16)
+
+    for step in range(STEPS):
+        state = st[step].reshape(n * rows, block).astype(jnp.float32)
+        xs[...] = (state * gain_ref[...]).astype(jnp.bfloat16)
+        squares = jnp.sum(state * state, axis=-1, keepdims=True)
+        sn[step] = jnp.broadcast_to(squares, (n * rows, HD)).reshape(n, rows, HD)
+        for d in range(1, n):
+            g = ring(s, d)
+            send(sn.at[step].at[g], rn.at[step].at[s], nsem.at[step], g, s, t, g)
+        if step == 0:
+            qcopy.wait()
+
+        @pl.loop(0, block // TILE)
+        def _(j):
+            at_cols = pl.ds(pl.multiple_of(j * TILE, TILE), TILE)
+            acc = jnp.dot(xs[...], qw[:, at_cols], preferred_element_type=jnp.float32)
+            sq[step, :, :, at_cols] = acc.astype(jnp.bfloat16).reshape(n, rows, TILE)
+
+        for d in range(1, n):
+            g = ring(s, d)
+            send(sq.at[step].at[g], rq.at[step].at[s], qsem.at[step], g, s, t, g)
+        total = sq[step, s].astype(jnp.float32)
+        norms = sn[step, s]
+        for d in range(1, n):
+            g = ring(s, d)
+            receive(rn.at[step].at[g], nsem.at[step], g)
+            receive(rq.at[step].at[g], qsem.at[step], g)
+            total += rq[step, g].astype(jnp.float32)
+            norms += rn[step, g]
+        scale = lax.rsqrt(norms[:, :1] * (1.0 / width) + EPSILON)
+        for h in range(block // HD):
+            head = total[:, h * HD : (h + 1) * HD] * scale
+            mean = jnp.mean(head * head, axis=-1, keepdims=True)
+            qn[step, :, h * HD : (h + 1) * HD] = (
+                head * lax.rsqrt(mean + EPSILON) * qgain_ref[...]
+            ).astype(jnp.bfloat16)
+        for d in range(1, n):
+            send(qn.at[step], aq.at[step].at[s], asem.at[step], d, s, ring(t, d), t)
+        send_or_keep(qn.at[step], aq.at[step].at[s], asem.at[step], 0, s, t, t)
+
+        position = t * toks + lax.broadcasted_iota(jnp.int32, (1, toks), 1)
+        lane = lax.broadcasted_iota(jnp.int32, (rows, HD), 1)
+        for d in (1, 2, 3, 0) if n == 4 else range(n - 1, -1, -1):
+            r = ring(s, d)
+            if d:
+                receive(aq.at[step].at[r], asem.at[step], r)
+            else:
+                receive_or_kept(aq.at[step].at[r], asem.at[step], r)
+            live = position < lens_ref[r]
+            sums = jnp.zeros((rows, HD), jnp.float32)
+            for j in range(kv):
+                cols = slice(j * HD, (j + 1) * HD)
+                heads = [
+                    aq[step, r, :, (j * GROUP + g) * HD : (j * GROUP + g + 1) * HD]
+                    for g in range(GROUP)
+                ]
+                scores = lax.dot_general(
+                    jnp.concatenate(heads, axis=0),
+                    keys_ref[r, :, cols],
+                    (((1,), (1,)), ((), ())),
+                    preferred_element_type=jnp.float32,
+                )
+                raw = jnp.where(live, jnp.exp(scores), 0.0)
+                total_raw = jnp.sum(raw, axis=-1, keepdims=True)
+                mixed = jnp.dot(
+                    raw.astype(jnp.bfloat16),
+                    values_ref[r, :, cols],
+                    preferred_element_type=jnp.float32,
+                ).astype(jnp.bfloat16)
+                for g in range(GROUP):
+                    h = j * GROUP + g
+                    span = slice(g * rows, (g + 1) * rows)
+                    so[step, r, :, h * HD : (h + 1) * HD] = mixed[span]
+                    sums = jnp.where(lane == h, total_raw[span], sums)
+            sl[step, r] = sums
+            put = send if d else send_or_keep
+            put(sl.at[step].at[r], rl.at[step].at[t], lsem.at[step], d, t, s, r)
+            put(so.at[step].at[r], ro.at[step].at[t], osem.at[step], d, t, s, r)
+        for d in (1, 2, 3, 0) if n == 4 else range(n - 1, -1, -1):
+            i = ring(t, d)
+            get = receive if d else receive_or_kept
+            get(rl.at[step].at[i], lsem.at[step], i)
+            get(ro.at[step].at[i], osem.at[step], i)
+        sums = rl[step, 0]
+        for i in range(1, n):
+            sums += rl[step, i]
+        for h in range(block // HD):
+            cols = slice(h * HD, (h + 1) * HD)
+            mixed = ro[step, 0, :, cols].astype(jnp.float32)
+            for i in range(1, n):
+                mixed += ro[step, i, :, cols].astype(jnp.float32)
+            at[step, :, cols] = (mixed / sums[:, h : h + 1]).astype(jnp.bfloat16)
+        for d in range(1, n):
+            g = ring(s, d)
+            send(at.at[step], aa.at[step].at[s], gsem.at[step], g, s, t, g)
+        aa[step, s] = at[step]
+        if step == 0:
+            ocopy.wait()
+        for d in range(1, n):
+            g = ring(s, d)
+            receive(aa.at[step].at[g], gsem.at[step], g)
+
+        @pl.loop(0, block // TILE)
+        def _(j):
+            at_cols = pl.ds(pl.multiple_of(j * TILE, TILE), TILE)
+            acc = jnp.dot(
+                aa[step].reshape(n * rows, block), ow[:, at_cols], preferred_element_type=jnp.float32
+            )
+            sb[step, :, :, at_cols] = acc.astype(jnp.bfloat16).reshape(n, rows, TILE)
+
+        for d in (2, 1, 3) if n == 4 else range(1, n):
+            i = ring(t, d)
+            send(sb.at[step].at[i], rb.at[step].at[t], bsem.at[step], i, t, i, s)
+        branch = sb[step, t].astype(jnp.float32)
+        for d in range(1, n):
+            i = ring(t, d)
+            receive(rb.at[step].at[i], bsem.at[step], i)
+            branch += rb[step, i].astype(jnp.float32)
+        live_row = lax.broadcasted_iota(jnp.int32, (rows, 1), 0) < rows_ref[t]
+        old = st[step, t].astype(jnp.float32)
+        st[step + 1, t] = (old + jnp.where(live_row, branch, 0.0)).astype(jnp.bfloat16)
+        for d in range(1, n):
+            i = ring(t, d)
+            send(st.at[step + 1].at[t], st.at[step + 1].at[t], ssem.at[step], i, t, i, s)
+        for d in range(1, n):
+            i = ring(t, d)
+            receive(st.at[step + 1].at[i], ssem.at[step], i)
+
+    for d in (1, 2, 3, 0) if n == 4 else range(n - 1, -1, -1):
+        g = ring(s, d)
+        for c in range(cap):
+            held = jnp.zeros((rows, block), jnp.float32)
+            for r in range(n):
+                chosen = map_ref[g, c * n + r] > 0
+                held = jnp.where(chosen, st[STEPS, r].astype(jnp.float32), held)
+            ob[g, c] = held.astype(jnp.bfloat16)
+        if d:
+            send(ob.at[g], rob.at[s], fsem, g, s, t, g)
+    rob[s] = ob[s]
+    for d in range(1, n):
+        g = ring(s, d)
+        receive(rob.at[g], fsem, g)
+    for c in range(cap):
+        occupied = map_ref[s, c * n] + map_ref[s, c * n + 1]
+        for r in range(2, n):
+            occupied += map_ref[s, c * n + r]
+        for g in range(n):
+            cols = slice(g * block, (g + 1) * block)
+            out_ref[c, :, cols] = jnp.where(
+                occupied > 0,
+                rob[g, c].astype(jnp.float32),
+                hidden_ref[c, :, cols].astype(jnp.float32),
+            ).astype(jnp.bfloat16)
+    for copy, when in sends:
+        if when is None:
+            copy.wait_send()
+        else:
+            pl.when(when)(copy.wait_send)
+
+
+def decode(n, lens, row_counts, slot_map, hidden, gain, q_gain, keys, values, q_weight, o_weight):
+    cap, rows, width = hidden.shape
+    block = width // n
+    bf, f32 = jnp.bfloat16, jnp.float32
+    vmem, smem = (pl.BlockSpec(memory_space=m) for m in (pltpu.VMEM, pltpu.SMEM))
+    hbm = pl.BlockSpec(memory_space=pl.ANY)
+    big, one = (STEPS, n, rows, block), (STEPS, rows, block)
+    small = (STEPS, n, rows, HD)
+    scratch = [
+        pltpu.VMEM(q_weight.shape, bf),
+        pltpu.VMEM(o_weight.shape, bf),
+        pltpu.VMEM((n * rows, block), bf),
+        pltpu.VMEM((n, cap, rows, block), bf),
+        pltpu.VMEM((STEPS + 1, n, rows, block), bf),
+        pltpu.VMEM(big, bf),
+        pltpu.VMEM(big, bf),
+        pltpu.VMEM(small, f32),
+        pltpu.VMEM(small, f32),
+        pltpu.VMEM(one, bf),
+        pltpu.VMEM(big, bf),
+        pltpu.VMEM(big, bf),
+        pltpu.VMEM(big, bf),
+        pltpu.VMEM(small, f32),
+        pltpu.VMEM(small, f32),
+        pltpu.VMEM(one, bf),
+        pltpu.VMEM(big, bf),
+        pltpu.VMEM(big, bf),
+        pltpu.VMEM(big, bf),
+        pltpu.VMEM((n, cap, rows, block), bf),
+        pltpu.VMEM((n, cap, rows, block), bf),
+        pltpu.SemaphoreType.DMA((2,)),
+        pltpu.SemaphoreType.DMA((2, n)),
+    ]
+    scratch += [pltpu.SemaphoreType.DMA((STEPS, 2, n))] * 8
+    scratch += [pltpu.SemaphoreType.DMA((2, n))]
+    return pl.pallas_call(
+        functools.partial(decode_kernel, n),
+        out_shape=jax.ShapeDtypeStruct(hidden.shape, bf),
+        in_specs=[smem] * 3 + [vmem] * 5 + [hbm] * 2,
+        out_specs=vmem,
+        scratch_shapes=scratch,
+        compiler_params=pltpu.CompilerParams(
+            collective_id=0, has_side_effects=True, vmem_limit_bytes=VMEM_LIMIT
+        ),
+        name="decode",
+    )(lens, row_counts, slot_map, hidden, gain, q_gain, keys, values, q_weight, o_weight)
+
+
+def square_body(
+    memory,
+    mem_lengths,
+    decode_group,
+    row_counts,
+    hidden,
+    norm_gain,
+    q_weight,
+    k_weight,
+    v_weight,
+    q_gain,
+    k_gain,
+    o_weight,
+):
+    n = lax.axis_size("tp")
+    req_count, tok_local, model_width = memory.shape
+    capacity = hidden.shape[0]
+    mem_rows = memory.reshape(req_count * tok_local, model_width)
+    key_acc = jnp.dot(
+        mem_rows,
+        lax.all_gather(k_weight, "tp", axis=0, tiled=True),
+        preferred_element_type=jnp.float32,
+    )
+    value_acc = jnp.dot(
+        mem_rows,
+        lax.all_gather(v_weight, "tp", axis=0, tiled=True),
+        preferred_element_type=jnp.float32,
+    )
+    keys = head_norm(key_acc.reshape(req_count, tok_local, -1, HD), k_gain)
+    keys = keys.astype(jnp.bfloat16).reshape(req_count, tok_local, -1)
+    values = value_acc.astype(jnp.bfloat16).reshape(req_count, tok_local, -1)
+    slot_map = slot_onehot(decode_group, n, capacity).astype(jnp.int32)
+    block = model_width // n
+    gain = lax.dynamic_slice_in_dim(norm_gain, lax.axis_index("section") * block, block)
+    return decode(
+        n,
+        mem_lengths,
+        row_counts,
+        slot_map.reshape(n, capacity * req_count),
+        hidden,
+        gain.astype(jnp.float32)[None, :],
+        (q_gain * HD ** (-0.5))[None, :],
+        keys,
+        values,
+        q_weight,
+        o_weight,
+    )
 
 
 def body(
@@ -151,4 +541,13 @@
         P("tp", "section"),
     )
     out_specs = P(("parts", "section"), None, None)
-    return jax.shard_map(body, mesh=mesh, in_specs=in_specs, out_specs=out_specs, check_vma=False)
+    square = mesh.shape["tp"] == mesh.shape["section"]
+
+    def whole(memory, *rest):
+        requests = memory.shape[0] // mesh.shape["parts"]
+        form = square_body if square and requests == mesh.shape["tp"] else body
+        return jax.shard_map(
+            form, mesh=mesh, in_specs=in_specs, out_specs=out_specs, check_vma=False
+        )(memory, *rest)
+
+    return whole

time: 834 us -> 378 us (0.45)
  waiting for transfers between devices: 602 us -> 144 us
  Pallas kernels: 0 us -> 181 us
  matrix products: 92 us -> 22.5 us
  blocking collectives: 51.9 us -> 0 us
  local copies, waits for them, and re-layouts: 61.6 us -> 9.9 us
    all_gather x4 -> x2, waiting for transfers between devices: 380 us -> 143 us  [the longest x1 79.7 us: square_body(): lax.all_gather(k_weight, 'tp', axis=0, tiled=True)]
    pallas_call x0 -> x1, Pallas kernels: none -> 181 us  [decode(): pl.pallas_call(functools.partial(decode_kernel, n), out_shape=jax.ShapeDt...]
    psum x2 -> x0, waiting for transfers between devices: 172 us -> none  [body(): lax.psum(jnp.dot(attended, o_full, preferred_element_type=jnp.float32), '...]
    dot_general x11 -> x2, matrix products: 92 us -> 22.5 us  [the longest x1 12.2 us: square_body(): jnp.dot(mem_rows, lax.all_gather(v_weight, 'tp', axis=0, tiled=True), pre...]
    all_to_all x1 -> x0, blocking collectives: 51.9 us -> none  [body(): lax.all_to_all(outgoing, 'section', split_axis=0, concat_axis=1, tiled=True)]
    dot_general x3 -> x1, local copies, waits for them, and re-layouts: 55 us -> 6.44 us  [square_body(): jnp.dot(mem_rows, lax.all_gather(k_weight, 'tp', axis=0, tiled=True), pre...]
    all_to_all x1 -> x0, waiting for transfers between devices: 47.3 us -> none  [body(): lax.all_to_all(spread, 'tp', split_axis=0, concat_axis=3, tiled=True)[0]]
  transfers between devices with their start and end apart: 7 -> 2, of which waited for: 7 -> 2; matrix products, arithmetic and copies ran while one was open for 13% -> 6% of each run, Pallas kernels for 0% -> 0%
where the time goes in v1:
time: 378 us; the launch traced here: 375 us
  Pallas kernels  181 us (48%)
  waiting for transfers between devices  144 us (38%)
  matrix products  22.5 us (6%)
  between operations  13.5 us (4%)
  local copies, waits for them, and re-layouts  9.9 us (3%)
  other arithmetic  4.71 us (1%)
    pallas_call x1, Pallas kernels, decode(): pl.pallas_call(functools.partial(decode_kernel, n), out_shape=jax.ShapeDt...  181 us
    all_gather x1, waiting for transfers between devices, square_body(): lax.all_gather(k_weight, 'tp', axis=0, tiled=True)  79.7 us
    all_gather x1, waiting for transfers between devices, square_body(): lax.all_gather(v_weight, 'tp', axis=0, tiled=True)  63 us
    dot_general x1, matrix products, square_body(): jnp.dot(mem_rows, lax.all_gather(v_weight, 'tp', axis=0, tiled=True), pre...  12.2 us
    dot_general x1, matrix products, square_body(): jnp.dot(mem_rows, lax.all_gather(k_weight, 'tp', axis=0, tiled=True), pre...  10.2 us
  transfers between devices with their start and end apart: 2, of which 2 were waited for; matrix products, arithmetic and copies ran while one was open for 6% of the time, Pallas kernels for 0%

profile of v1, /device:TPU:0, one launch (start us, length us, event | category | flops | bytes accessed | tf_op | source)
XLA Modules:
  0.0 375.3 jit_solution(1550333044520494049)
XLA Ops:
  6.5 0.0 all-gather.3.cloned.1.call-start
  6.5 0.7 all-gather.3.cloned.1.call-update
  7.3 0.0 all-gather.5.cloned.1.call-start
  7.3 0.7 all-gather.5.cloned.1.call-update
  8.0 0.8 convert_reduce_fusion
  8.8 0.1 eq.58
  8.9 0.7 iota_compare_fusion.1
  9.7 0.1 copy.13
  9.8 1.3 dynamic-slice_convert_fusion
  11.0 1.2 multiply_bitcast_fusion.qgain_ref
  12.2 0.6 convert_convert_fusion.map_ref
  12.8 79.7 %all-gather.3.cloned.1.call-done = bf16[8192,256]{1,0:T(8,128)(2,1)} async-done(((bf16[2048,256]{1,0:T(8,128)(2,1)}), bf16[8192,256]{1,0:T(8,128)(2,1)}) %all-gather.3.cloned.1.call-update) | async-done | bytes 4194320 | tf_op jit(solution)/shard_map/all_gather | solution.py:397
  92.4 6.4 %copy.14 = bf16[256,8192]{1,0:T(8,128)(2,1)} copy(bf16[256,8192]{0,1:T(8,128)(2,1)} %bitcast.21) | data formatting | bytes 8388608 | tf_op jit(solution)/shard_map/dot_general | solution.py:395
  98.9 0.0 copy-start
  98.9 10.2 %multiply_reduce_fusion = (f32[4,256,2]{1,2,0:T(2,128)S(1)}, f32[4,256,2,128]{1,3,2,0:T(8,128)S(1)}) fusion(bf16[2,128,8192,1]{2,1,0,3:T(8,128)(2,1)} %bitcast.22, bf16[4,256,8192]{2,1,0:T(8,128)(2,1)} %param.12), kind=kOutput, calls=%fused_computation.4 | convolution fusion | flops 4295489536 | bytes 22028288 | tf_op jit(solution)/shard_map/dot_general | solution.py:395
  109.1 0.0 copy-done
  109.1 0.1 multiply_convert_fusion
  109.3 1.0 copy.17.keys_ref
  110.3 63.0 %all-gather.5.cloned.1.call-done = bf16[8192,256]{1,0:T(8,128)(2,1)} async-done(((bf16[2048,256]{1,0:T(8,128)(2,1)}), bf16[8192,256]{1,0:T(8,128)(2,1)}) %all-gather.5.cloned.1.call-update) | async-done | bytes 4194320 | tf_op jit(solution)/shard_map/all_gather | solution.py:402
  173.3 12.2 %convolution_convert_fusion = bf16[1024,256]{1,0:T(8,128)(2,1)} fusion(bf16[1024,8192]{1,0:T(8,128)(2,1)} %bitcast.26, bf16[8192,256]{1,0:T(8,128)(2,1)} %all-gather.5.cloned.1.call-done), kind=kOutput, calls=%fused_computation.2 | convolution fusion | flops 4295229440 | bytes 21495808 | tf_op jit(solution)/shard_map/dot_general | solution.py:400
  185.6 180.7 %decode.1 = bf16[2,32,8192]{2,1,0:T(8,128)(2,1)} custom-call(s32[4]{0:T(128)} %lens_ref.1, s32[4]{0:T(128)} %rows_ref.1, s32[4,8]{1,0:T(4,128)} %convert_convert_fusion.map_ref, bf16[2,32,8192]{2,1,0:T(8,128)(2,1)} %hidden_ref.1, f32[1,2048]{1,0:T(1,128)} %bitcast.25, f32[1,128]{1,0:T(1,128)} %multiply_bitcast_fusion.qgain_ref, ...), custom_call_target="tpu_custom_call" | custom-call | tf_op jit(solution)/shard_map/decode/pallas_call | solution.py:364
  366.2 2.3 copy.19
  (3 shorter events, 0.0 us)
Async XLA Ops:
  6.5 85.9 %all-gather.3.cloned.1.call-start = ((), (), s32[]{:S(2)}) async-start(), calls=%async_computation | async-start | bytes 5242880 | tf_op jit(solution)/shard_map/all_gather | solution.py:397
  7.3 166.1 %all-gather.5.cloned.1.call-start = ((), (), s32[]{:S(2)}) async-start(), calls=%async_computation.1 | async-start | bytes 5242880 | tf_op jit(solution)/shard_map/all_gather | solution.py:402
  98.9 10.3 %copy-start = (f32[128]{0:T(128)S(1)}, f32[128]{0:T(128)}, u32[]{:S(2)}) copy-start(f32[128]{0:T(128)} %param.22) | copy-start | bytes 1540
Sparse Core Ops, SparseCore 0:
  8.9 83.4 all-gather.2
  94.0 79.2 all-gather.4

commit v2 on v1

--- a/solution.py
+++ b/solution.py
@@ -16,7 +16,9 @@
 EPSILON = 1e-06
 MESH = pl.DeviceIdType.MESH
 TILE = 512
-VMEM_LIMIT = 58 * 1024 * 1024
+VMEM_LIMIT = 60 * 1024 * 1024
+SUB = 2
+ROW_TILE = 256
 
 
 def head_norm(values_in, gain_vector):
@@ -48,13 +50,19 @@
     hidden_ref,
     gain_ref,
     qgain_ref,
-    keys_ref,
-    values_ref,
+    kgain_ref,
+    mem_hbm,
+    kw_hbm,
+    vw_hbm,
     qw_hbm,
     ow_hbm,
     out_ref,
+    mem,
+    wkv,
+    acc_kv,
+    keys_ref,
+    values_ref,
     qw,
-    ow,
     xs,
     hb,
     st,
@@ -85,6 +93,12 @@
     bsem,
     ssem,
     fsem,
+    msem,
+    lwsem,
+    upsem,
+    dnsem,
+    zsem,
+    ysem,
 ):
     part = lax.axis_index("parts")
     t = lax.axis_index("tp")
@@ -93,6 +107,9 @@
     block = width // n
     toks = keys_ref.shape[1]
     kv = keys_ref.shape[2] // HD
+    peer = 1 - part
+    sub_rows = wkv.shape[4]
+    half_block = mem.shape[2]
     diag = s == t
     sends = []
 
@@ -137,8 +154,6 @@
 
     qcopy = pltpu.make_async_copy(qw_hbm, qw, wsem.at[0])
     qcopy.start()
-    ocopy = pltpu.make_async_copy(ow_hbm, ow, wsem.at[1])
-    ocopy.start()
 
     barrier = pltpu.get_barrier_semaphore()
     for dt in range(n):
@@ -147,7 +162,106 @@
                 pl.semaphore_signal(
                     barrier, inc=1, device_id=(part, ring(t, dt), ring(s, ds)), device_id_type=MESH
                 )
-    pl.semaphore_wait(barrier, n * n - 1)
+    pl.semaphore_signal(barrier, inc=1, device_id=(peer, t, s), device_id_type=MESH)
+    pl.semaphore_wait(barrier, n * n)
+
+    pieces = [(w, u) for w in range(2) for u in range(SUB)]
+
+    def move(src, dst, send_sem, recv_sem, part_to, tp_to):
+        return pltpu.make_async_remote_copy(
+            src_ref=src,
+            dst_ref=dst,
+            send_sem=send_sem,
+            recv_sem=recv_sem,
+            device_id=(part_to, tp_to, s),
+            device_id_type=MESH,
+        )
+
+    def start_if(copy, when):
+        pl.when(when)(copy.start)
+        sends.append((copy, when))
+
+    above, below = t < n - 1, t > 0
+    up, down = lax.rem(t + 1, n), lax.rem(t + n - 1, n)
+    for c, (w, u) in enumerate(pieces):
+        first = pl.multiple_of((part * SUB + u) * sub_rows, sub_rows)
+        src = (kw_hbm, vw_hbm)[w].at[pl.ds(first, sub_rows), :]
+        dst = wkv.at[t, w, part, u]
+        start_if(move(src, dst, upsem.at[t, c], zsem.at[t, c], part, up), above)
+        start_if(move(src, dst, dnsem.at[t, c], zsem.at[t, c], part, down), below)
+
+    own_copies = [
+        pltpu.make_async_copy(
+            (kw_hbm, vw_hbm)[w].at[pl.ds((q * SUB + u) * sub_rows, sub_rows), :],
+            wkv.at[t, w, q, u],
+            lwsem.at[w, q, u],
+        )
+        for w in range(2)
+        for q in range(2)
+        for u in range(SUB)
+    ]
+    for copy in own_copies:
+        copy.start()
+
+    def mem_copies(i):
+        return [
+            pltpu.make_async_copy(
+                mem_hbm.at[:, pl.ds(pl.multiple_of(i * block + k * half_block, half_block), half_block)],
+                mem.at[2 * i + k],
+                msem.at[i, k],
+            )
+            for k in range(2)
+        ]
+
+    for d in range(n):
+        for copy in mem_copies(ring(t, d)):
+            copy.start()
+
+    def project(i, fresh):
+        for copy in mem_copies(i):
+            copy.wait()
+
+        @pl.loop(0, mem.shape[1] // ROW_TILE)
+        def _(j):
+            at_rows = pl.ds(pl.multiple_of(j * ROW_TILE, ROW_TILE), ROW_TILE)
+            for w in range(2):
+                acc = jnp.zeros((ROW_TILE, kv * HD), jnp.float32) if fresh else acc_kv[w, at_rows, :]
+                for k in range(2):
+                    acc += jnp.dot(
+                        mem[2 * i + k, at_rows, :],
+                        wkv[i, w, k].reshape(half_block, kv * HD),
+                        preferred_element_type=jnp.float32,
+                    )
+                acc_kv[w, at_rows, :] = acc
+
+    def arrivals(d):
+        yield ring(t, n - d), t - d >= 0, up, above, upsem
+        yield ring(t, d), t + d < n, down, below, dnsem
+
+    def relay(d):
+        for c, (w, u) in enumerate(pieces):
+            for i, here, onward, further, out_sem in arrivals(d):
+                piece = wkv.at[i, w, part, u]
+
+                @pl.when(here)
+                def _():
+                    move(piece, piece, out_sem.at[i, c], zsem.at[i, c], part, t).wait_recv()
+
+                start_if(
+                    move(piece, piece, out_sem.at[i, c], zsem.at[i, c], part, onward),
+                    jnp.logical_and(here, further),
+                )
+                start_if(move(piece, piece, ysem.at[0, i, c], ysem.at[1, i, c], peer, t), here)
+
+    def absorb(d):
+        for i, here, _, _, _ in arrivals(d):
+
+            @pl.when(here)
+            def _():
+                for c, (w, u) in enumerate(pieces):
+                    piece = wkv.at[i, w, peer, u]
+                    move(piece, piece, ysem.at[0, i, c], ysem.at[1, i, c], peer, t).wait_recv()
+                project(i, False)
 
     def columns(i):
         return pl.ds(pl.multiple_of(i * block, block), block)
@@ -156,6 +270,9 @@
         g = ring(s, d)
         send(hidden_ref.at[:, :, columns(g)], hb.at[s], hsem, g, s, t, g)
     hb[s] = hidden_ref[:, :, columns(s)]
+    for copy in own_copies:
+        copy.wait()
+    project(t, True)
     for d in range(1, n):
         g = ring(s, d)
         receive(hb.at[g], hsem, g)
@@ -187,6 +304,8 @@
         for d in range(1, n):
             g = ring(s, d)
             send(sq.at[step].at[g], rq.at[step].at[s], qsem.at[step], g, s, t, g)
+        if step == 0:
+            relay(1)
         total = sq[step, s].astype(jnp.float32)
         norms = sn[step, s]
         for d in range(1, n):
@@ -205,6 +324,35 @@
         for d in range(1, n):
             send(qn.at[step], aq.at[step].at[s], asem.at[step], d, s, ring(t, d), t)
         send_or_keep(qn.at[step], aq.at[step].at[s], asem.at[step], 0, s, t, t)
+
+        if step == 0:
+            for d in range(2, n):
+                absorb(d - 1)
+                relay(d)
+            absorb(n - 1)
+            ocopies = [
+                pltpu.make_async_copy(
+                    ow_hbm.at[
+                        pl.ds(k * half_block, half_block), pl.ds(c * half_block, half_block)
+                    ],
+                    mem.at[2 * k + c],
+                    wsem.at[1 + 2 * k + c],
+                )
+                for c in range(2)
+                for k in range(2)
+            ]
+            for copy in ocopies:
+                copy.start()
+
+            @pl.loop(0, n)
+            def _(r):
+                at_rows = pl.ds(pl.multiple_of(r * toks, toks), toks)
+                for j in range(kv):
+                    cols = slice(j * HD, (j + 1) * HD)
+                    keys_ref[r, :, cols] = head_norm(acc_kv[0, at_rows, cols], kgain_ref[...]).astype(
+                        jnp.bfloat16
+                    )
+                values_ref[r] = acc_kv[1, at_rows, :].astype(jnp.bfloat16)
 
         position = t * toks + lax.broadcasted_iota(jnp.int32, (1, toks), 1)
         lane = lax.broadcasted_iota(jnp.int32, (rows, HD), 1)
@@ -263,18 +411,29 @@
             send(at.at[step], aa.at[step].at[s], gsem.at[step], g, s, t, g)
         aa[step, s] = at[step]
         if step == 0:
-            ocopy.wait()
+            for copy in ocopies:
+                copy.wait()
         for d in range(1, n):
             g = ring(s, d)
             receive(aa.at[step].at[g], gsem.at[step], g)
 
-        @pl.loop(0, block // TILE)
-        def _(j):
-            at_cols = pl.ds(pl.multiple_of(j * TILE, TILE), TILE)
-            acc = jnp.dot(
-                aa[step].reshape(n * rows, block), ow[:, at_cols], preferred_element_type=jnp.float32
-            )
-            sb[step, :, :, at_cols] = acc.astype(jnp.bfloat16).reshape(n, rows, TILE)
+        for c in range(2):
+
+            @pl.loop(0, half_block // TILE)
+            def _(j):
+                in_cols = pl.ds(pl.multiple_of(j * TILE, TILE), TILE)
+                at_cols = pl.ds(pl.multiple_of(c * half_block + j * TILE, TILE), TILE)
+                mixed_rows = aa[step].reshape(n * rows, block)
+                acc = jnp.dot(
+                    mixed_rows[:, :half_block],
+                    mem[c, :, in_cols],
+                    preferred_element_type=jnp.float32,
+                ) + jnp.dot(
+                    mixed_rows[:, half_block:],
+                    mem[2 + c, :, in_cols],
+                    preferred_element_type=jnp.float32,
+                )
+                sb[step, :, :, at_cols] = acc.astype(jnp.bfloat16).reshape(n, rows, TILE)
 
         for d in (2, 1, 3) if n == 4 else range(1, n):
             i = ring(t, d)
@@ -326,17 +485,36 @@
             pl.when(when)(copy.wait_send)
 
 
-def decode(n, lens, row_counts, slot_map, hidden, gain, q_gain, keys, values, q_weight, o_weight):
+def decode(
+    n,
+    lens,
+    row_counts,
+    slot_map,
+    hidden,
+    gain,
+    q_gain,
+    k_gain,
+    mem_rows,
+    k_weight,
+    v_weight,
+    q_weight,
+    o_weight,
+):
     cap, rows, width = hidden.shape
     block = width // n
+    feats = k_weight.shape[1]
     bf, f32 = jnp.bfloat16, jnp.float32
     vmem, smem = (pl.BlockSpec(memory_space=m) for m in (pltpu.VMEM, pltpu.SMEM))
     hbm = pl.BlockSpec(memory_space=pl.ANY)
     big, one = (STEPS, n, rows, block), (STEPS, rows, block)
     small = (STEPS, n, rows, HD)
     scratch = [
+        pltpu.VMEM((2 * n, mem_rows.shape[0], block // 2), bf),
+        pltpu.VMEM((n, 2, 2, SUB, block // 2 // SUB, feats), bf),
+        pltpu.VMEM((2, mem_rows.shape[0], feats), f32),
+        pltpu.VMEM((n, mem_rows.shape[0] // n, feats), bf),
+        pltpu.VMEM((n, mem_rows.shape[0] // n, feats), bf),
         pltpu.VMEM(q_weight.shape, bf),
-        pltpu.VMEM(o_weight.shape, bf),
         pltpu.VMEM((n * rows, block), bf),
         pltpu.VMEM((n, cap, rows, block), bf),
         pltpu.VMEM((STEPS + 1, n, rows, block), bf),
@@ -356,22 +534,43 @@
         pltpu.VMEM(big, bf),
         pltpu.VMEM((n, cap, rows, block), bf),
         pltpu.VMEM((n, cap, rows, block), bf),
-        pltpu.SemaphoreType.DMA((2,)),
+        pltpu.SemaphoreType.DMA((5,)),
         pltpu.SemaphoreType.DMA((2, n)),
     ]
     scratch += [pltpu.SemaphoreType.DMA((STEPS, 2, n))] * 8
-    scratch += [pltpu.SemaphoreType.DMA((2, n))]
+    scratch += [
+        pltpu.SemaphoreType.DMA((2, n)),
+        pltpu.SemaphoreType.DMA((n, 2)),
+        pltpu.SemaphoreType.DMA((2, 2, SUB)),
+        pltpu.SemaphoreType.DMA((n, 2 * SUB)),
+        pltpu.SemaphoreType.DMA((n, 2 * SUB)),
+        pltpu.SemaphoreType.DMA((n, 2 * SUB)),
+        pltpu.SemaphoreType.DMA((2, n, 2 * SUB)),
+    ]
     return pl.pallas_call(
         functools.partial(decode_kernel, n),
         out_shape=jax.ShapeDtypeStruct(hidden.shape, bf),
-        in_specs=[smem] * 3 + [vmem] * 5 + [hbm] * 2,
+        in_specs=[smem] * 3 + [vmem] * 4 + [hbm] * 5,
         out_specs=vmem,
         scratch_shapes=scratch,
         compiler_params=pltpu.CompilerParams(
             collective_id=0, has_side_effects=True, vmem_limit_bytes=VMEM_LIMIT
         ),
         name="decode",
-    )(lens, row_counts, slot_map, hidden, gain, q_gain, keys, values, q_weight, o_weight)
+    )(
+        lens,
+        row_counts,
+        slot_map,
+        hidden,
+        gain,
+        q_gain,
+        k_gain,
+        mem_rows,
+        k_weight,
+        v_weight,
+        q_weight,
+        o_weight,
+    )
 
 
 def square_body(
@@ -392,19 +591,6 @@
     req_count, tok_local, model_width = memory.shape
     capacity = hidden.shape[0]
     mem_rows = memory.reshape(req_count * tok_local, model_width)
-    key_acc = jnp.dot(
-        mem_rows,
-        lax.all_gather(k_weight, "tp", axis=0, tiled=True),
-        preferred_element_type=jnp.float32,
-    )
-    value_acc = jnp.dot(
-        mem_rows,
-        lax.all_gather(v_weight, "tp", axis=0, tiled=True),
-        preferred_element_type=jnp.float32,
-    )
-    keys = head_norm(key_acc.reshape(req_count, tok_local, -1, HD), k_gain)
-    keys = keys.astype(jnp.bfloat16).reshape(req_count, tok_local, -1)
-    values = value_acc.astype(jnp.bfloat16).reshape(req_count, tok_local, -1)
     slot_map = slot_onehot(decode_group, n, capacity).astype(jnp.int32)
     block = model_width // n
     gain = lax.dynamic_slice_in_dim(norm_gain, lax.axis_index("section") * block, block)
@@ -416,8 +602,10 @@
         hidden,
         gain.astype(jnp.float32)[None, :],
         (q_gain * HD ** (-0.5))[None, :],
-        keys,
-        values,
+        k_gain[None, :],
+        mem_rows,
+        k_weight,
+        v_weight,
         q_weight,
         o_weight,
     )
@@ -541,11 +729,13 @@
         P("tp", "section"),
     )
     out_specs = P(("parts", "section"), None, None)
-    square = mesh.shape["tp"] == mesh.shape["section"]
 
     def whole(memory, *rest):
-        requests = memory.shape[0] // mesh.shape["parts"]
-        form = square_body if square and requests == mesh.shape["tp"] else body
+        parts, tp = mesh.shape["parts"], mesh.shape["tp"]
+        requests, tokens, width = memory.shape
+        square = parts == 2 and tp == mesh.shape["section"] and requests == parts * tp
+        square = square and 2 * requests * tokens == parts * width
+        form = square_body if square else body
         return jax.shard_map(
             form, mesh=mesh, in_specs=in_specs, out_specs=out_specs, check_vma=False
         )(memory, *rest)

time: 378 us -> 245 us (0.65)
  waiting for transfers between devices: 144 us -> 0 us
  Pallas kernels: 181 us -> 236 us
  matrix products: 22.5 us -> 0 us
  between operations: 13.5 us -> 0.01 us
  local copies, waits for them, and re-layouts: 9.9 us -> 2.45 us
    all_gather x2 -> x0, waiting for transfers between devices: 143 us -> none  [the longest x1 79.7 us: square_body(): lax.all_gather(k_weight, 'tp', axis=0, tiled=True)]
    pallas_call x1, Pallas kernels: 181 us -> 236 us  [decode(): pl.pallas_call(functools.partial(decode_kernel, n), out_shape=jax.ShapeDt...]
    dot_general x2 -> x0, matrix products: 22.5 us -> none  [the longest x1 12.2 us: square_body(): jnp.dot(mem_rows, lax.all_gather(v_weight, 'tp', axis=0, tiled=True), pre...]
    dot_general x1 -> x0, local copies, waits for them, and re-layouts: 6.44 us -> none  [square_body(): jnp.dot(mem_rows, lax.all_gather(k_weight, 'tp', axis=0, tiled=True), pre...]
  transfers between devices with their start and end apart: 2 -> 0, of which waited for: 2 -> 0; matrix products, arithmetic and copies ran while one was open for 6% -> 0% of each run, Pallas kernels for 0% -> 0%
where the time goes in v2:
time: 245 us; the launch traced here: 243 us
  Pallas kernels  236 us (96%)
  other arithmetic  4.6 us (2%)
  local copies, waits for them, and re-layouts  2.45 us (1%)
    pallas_call x1, Pallas kernels, decode(): pl.pallas_call(functools.partial(decode_kernel, n), out_shape=jax.ShapeDt...  236 us

profile of v2, /device:TPU:0, one launch (start us, length us, event | category | flops | bytes accessed | tf_op | source)
XLA Modules:
  0.0 242.7 jit_solution(7248890047358361211)
XLA Ops:
  0.0 1.2 multiply_bitcast_fusion.qgain_ref
  1.2 0.8 convert_reduce_fusion
  2.0 0.1 eq.58
  2.1 0.7 iota_compare_fusion.1
  2.8 0.1 copy.13
  2.9 0.6 convert_convert_fusion.map_ref
  3.5 1.3 dynamic-slice_convert_fusion
  4.8 235.7 %decode.1 = bf16[2,32,8192]{2,1,0:T(8,128)(2,1)} custom-call(s32[4]{0:T(128)} %lens_ref.1, s32[4]{0:T(128)} %rows_ref.1, s32[4,8]{1,0:T(4,128)} %convert_convert_fusion.map_ref, bf16[2,32,8192]{2,1,0:T(8,128)(2,1)} %hidden_ref.1, f32[1,2048]{1,0:T(1,128)} %bitcast.7, f32[1,128]{1,0:T(1,128)} %multiply_bitcast_fusion.qgain_ref, f32[1,128]{1,0:T(1,128)} %bitcast.8, ...), custom_call_target="tpu_custom_call" | custom-call | tf_op jit(solution)/shard_map/decode/pallas_call | solution.py:550
  240.5 2.3 copy.15
  (2 shorter events, 0.0 us)

commit v3 on v2

--- a/solution.py
+++ b/solution.py
@@ -73,8 +73,10 @@
     qn,
     aq,
     so,
+    xo,
     ro,
     sl,
+    xl,
     rl,
     at,
     aa,
@@ -87,6 +89,8 @@
     qsem,
     nsem,
     asem,
+    xosem,
+    xlsem,
     osem,
     lsem,
     gsem,
@@ -389,14 +393,26 @@
                     so[step, r, :, h * HD : (h + 1) * HD] = mixed[span]
                     sums = jnp.where(lane == h, total_raw[span], sums)
             sl[step, r] = sums
-            put = send if d else send_or_keep
-            put(sl.at[step].at[r], rl.at[step].at[t], lsem.at[step], d, t, s, r)
-            put(so.at[step].at[r], ro.at[step].at[t], osem.at[step], d, t, s, r)
+            if d:
+                send(sl.at[step].at[r], xl.at[step].at[s], xlsem.at[step], r, s, t, r)
+                send(so.at[step].at[r], xo.at[step].at[s], xosem.at[step], r, s, t, r)
+        xl[step, s] = sl[step, s]
+        xo[step, s] = so[step, s]
         for d in (1, 2, 3, 0) if n == 4 else range(n - 1, -1, -1):
+            h = ring(s, d)
+            if d:
+                receive(xl.at[step].at[h], xlsem.at[step], h)
+                receive(xo.at[step].at[h], xosem.at[step], h)
+            away = h != t
+            for src, dst, sems in ((xl, rl, lsem), (xo, ro, osem)):
+                piece, slot = src.at[step].at[h], dst.at[step].at[t]
+                start_if(remote(piece, slot, sems.at[step], h, t, h, s), away)
+        rl[step, t] = xl[step, t]
+        ro[step, t] = xo[step, t]
+        for d in range(1, n):
             i = ring(t, d)
-            get = receive if d else receive_or_kept
-            get(rl.at[step].at[i], lsem.at[step], i)
-            get(ro.at[step].at[i], osem.at[step], i)
+            receive(rl.at[step].at[i], lsem.at[step], i)
+            receive(ro.at[step].at[i], osem.at[step], i)
         sums = rl[step, 0]
         for i in range(1, n):
             sums += rl[step, i]
@@ -435,23 +451,38 @@
                 )
                 sb[step, :, :, at_cols] = acc.astype(jnp.bfloat16).reshape(n, rows, TILE)
 
-        for d in (2, 1, 3) if n == 4 else range(1, n):
-            i = ring(t, d)
-            send(sb.at[step].at[i], rb.at[step].at[t], bsem.at[step], i, t, i, s)
-        branch = sb[step, t].astype(jnp.float32)
-        for d in range(1, n):
-            i = ring(t, d)
-            receive(rb.at[step].at[i], bsem.at[step], i)
-            branch += rb[step, i].astype(jnp.float32)
+            cols = slice(c * half_block, (c + 1) * half_block)
+            for d in (2, 1, 3) if n == 4 else range(1, n):
+                i = ring(t, d)
+                send(
+                    sb.at[step, i, :, cols],
+                    rb.at[step, t, :, cols],
+                    bsem.at[2 * step + c],
+                    i,
+                    t,
+                    i,
+                    s,
+                )
+
         live_row = lax.broadcasted_iota(jnp.int32, (rows, 1), 0) < rows_ref[t]
-        old = st[step, t].astype(jnp.float32)
-        st[step + 1, t] = (old + jnp.where(live_row, branch, 0.0)).astype(jnp.bfloat16)
-        for d in range(1, n):
-            i = ring(t, d)
-            send(st.at[step + 1].at[t], st.at[step + 1].at[t], ssem.at[step], i, t, i, s)
-        for d in range(1, n):
-            i = ring(t, d)
-            receive(st.at[step + 1].at[i], ssem.at[step], i)
+        for c in range(2):
+            cols = slice(c * half_block, (c + 1) * half_block)
+            branch = sb[step, t, :, cols].astype(jnp.float32)
+            for d in range(1, n):
+                i = ring(t, d)
+                receive(rb.at[step, i, :, cols], bsem.at[2 * step + c], i)
+                branch += rb[step, i, :, cols].astype(jnp.float32)
+            old = st[step, t, :, cols].astype(jnp.float32)
+            st[step + 1, t, :, cols] = (old + jnp.where(live_row, branch, 0.0)).astype(jnp.bfloat16)
+            for d in range(1, n):
+                i = ring(t, d)
+                own = st.at[step + 1, t, :, cols]
+                send(own, own, ssem.at[2 * step + c], i, t, i, s)
+        for c in range(2):
+            cols = slice(c * half_block, (c + 1) * half_block)
+            for d in range(1, n):
+                i = ring(t, d)
+                receive(st.at[step + 1, i, :, cols], ssem.at[2 * step + c], i)
 
     for d in (1, 2, 3, 0) if n == 4 else range(n - 1, -1, -1):
         g = ring(s, d)
@@ -526,6 +557,8 @@
         pltpu.VMEM(big, bf),
         pltpu.VMEM(big, bf),
         pltpu.VMEM(big, bf),
+        pltpu.VMEM(big, bf),
+        pltpu.VMEM(small, f32),
         pltpu.VMEM(small, f32),
         pltpu.VMEM(small, f32),
         pltpu.VMEM(one, bf),
@@ -538,6 +571,7 @@
         pltpu.SemaphoreType.DMA((2, n)),
     ]
     scratch += [pltpu.SemaphoreType.DMA((STEPS, 2, n))] * 8
+    scratch += [pltpu.SemaphoreType.DMA((2 * STEPS, 2, n))] * 2
     scratch += [
         pltpu.SemaphoreType.DMA((2, n)),
         pltpu.SemaphoreType.DMA((n, 2)),

time: 245 us -> 237 us (0.967)
  Pallas kernels: 236 us -> 226 us
    pallas_call x1, Pallas kernels: 236 us -> 226 us  [decode(): pl.pallas_call(functools.partial(decode_kernel, n), out_shape=jax.ShapeDt...]
where the time goes in v3:
time: 237 us; the launch traced here: 233 us
  Pallas kernels  226 us (95%)
  other arithmetic  4.6 us (2%)
  local copies, waits for them, and re-layouts  2.45 us (1%)
    pallas_call x1, Pallas kernels, decode(): pl.pallas_call(functools.partial(decode_kernel, n), out_shape=jax.ShapeDt...  226 us

profile of v3, /device:TPU:0, one launch (start us, length us, event | category | flops | bytes accessed | tf_op | source)
XLA Modules:
  0.0 233.5 jit_solution(14550250581761597110)
XLA Ops:
  0.0 1.2 multiply_bitcast_fusion.qgain_ref
  1.2 0.8 convert_reduce_fusion
  2.0 0.1 eq.58
  2.1 0.7 iota_compare_fusion.1
  2.8 0.1 copy.13
  2.9 0.6 convert_convert_fusion.map_ref
  3.5 1.3 dynamic-slice_convert_fusion
  4.8 226.4 %decode.1 = bf16[2,32,8192]{2,1,0:T(8,128)(2,1)} custom-call(s32[4]{0:T(128)} %lens_ref.1, s32[4]{0:T(128)} %rows_ref.1, s32[4,8]{1,0:T(4,128)} %convert_convert_fusion.map_ref, bf16[2,32,8192]{2,1,0:T(8,128)(2,1)} %hidden_ref.1, f32[1,2048]{1,0:T(1,128)} %bitcast.7, f32[1,128]{1,0:T(1,128)} %multiply_bitcast_fusion.qgain_ref, f32[1,128]{1,0:T(1,128)} %bitcast.8, ...), custom_call_target="tpu_custom_call" | custom-call | tf_op jit(solution)/shard_map/decode/pallas_call | solution.py:584
  231.2 2.3 copy.15
  (2 shorter events, 0.0 us)

commit v4 on v3

--- a/solution.py
+++ b/solution.py
@@ -331,8 +331,8 @@
 
         if step == 0:
             for d in range(2, n):
+                relay(d)
                 absorb(d - 1)
-                relay(d)
             absorb(n - 1)
             ocopies = [
                 pltpu.make_async_copy(

time: 237 us -> 232 us (0.979)
    pallas_call x1, Pallas kernels: 226 us -> 224 us  [decode(): pl.pallas_call(functools.partial(decode_kernel, n), out_shape=jax.ShapeDt...]
where the time goes in v4:
time: 232 us; the launch traced here: 231 us
  Pallas kernels  224 us (97%)
  other arithmetic  4.6 us (2%)
  local copies, waits for them, and re-layouts  2.45 us (1%)
    pallas_call x1, Pallas kernels, decode(): pl.pallas_call(functools.partial(decode_kernel, n), out_shape=jax.ShapeDt...  224 us

profile of v4, /device:TPU:0, one launch (start us, length us, event | category | flops | bytes accessed | tf_op | source)
XLA Modules:
  0.0 230.7 jit_solution(15136526197945299535)
XLA Ops:
  0.0 1.2 multiply_bitcast_fusion.qgain_ref
  1.2 0.8 convert_reduce_fusion
  2.0 0.1 eq.58
  2.1 0.7 iota_compare_fusion.1
  2.8 0.1 copy.13
  2.9 0.6 convert_convert_fusion.map_ref
  3.5 1.3 dynamic-slice_convert_fusion
  4.8 223.6 %decode.1 = bf16[2,32,8192]{2,1,0:T(8,128)(2,1)} custom-call(s32[4]{0:T(128)} %lens_ref.1, s32[4]{0:T(128)} %rows_ref.1, s32[4,8]{1,0:T(4,128)} %convert_convert_fusion.map_ref, bf16[2,32,8192]{2,1,0:T(8,128)(2,1)} %hidden_ref.1, f32[1,2048]{1,0:T(1,128)} %bitcast.7, f32[1,128]{1,0:T(1,128)} %multiply_bitcast_fusion.qgain_ref, f32[1,128]{1,0:T(1,128)} %bitcast.8, ...), custom_call_target="tpu_custom_call" | custom-call | tf_op jit(solution)/shard_map/decode/pallas_call | solution.py:584
  228.4 2.3 copy.15
  (2 shorter events, 0.0 us)
